TPU v7x, 32 devices: a whole 2x2x4 slice. The times are simulated.
32 devices in a mesh: pool: 16 (over z, y, x), tensor: 2 (over core).
Axes of the slice: x: 2, y: 2, z: 4, core: 2. Of those that a mesh axis runs over, the one named last changes fastest.
Arguments:
- tokens: bfloat16 [2, 256, 8192], P(None, None, 'tensor'), may hold values from -6 to 6
- gate_up_weight: bfloat16 [8192, 2, 28672], P('tensor', None, 'pool'), may hold values from -0.0625 to 0.0625
- down_weight: bfloat16 [28672, 8192], P('pool', 'tensor'), may hold values from -0.03125 to 0.03125
- shrink_store: bfloat16 [16, 2, 8192, 64], P('pool', None, 'tensor'), may hold values from -0.0625 to 0.0625
- expand_store: bfloat16 [16, 2, 64, 28672], P('pool', None, 'tensor'), may hold values from -0.75 to 0.75
- block_adapter: int32 [2, 2], replicated, may hold values from 0 to 15
- block_live: int32 [2, 2], replicated, may hold values from 1 to 128, 192 in all within a row
- adapter_slot: int32 [16], replicated, may hold values from 0 to 15, each once
Outputs:
- layer_out: bfloat16 [2, 256, 8192], P(None, 'pool', 'tensor')
Inputs may be any that keep to these rules, and one draw needn't show every extreme that they name: Each storage slot holds exactly one adapter; adapter a is stored on index adapter_slot[a] of pool; each index of pool holds exactly one storage slot. `block_live`: rows of a block after its live rows are padding; the live rows of one decode step sum to 192.
All inputs are finite; a program needn't handle non-finite values.
Results may differ from a plain program's by a relative error of at most 0.0049.
Values may be sent and summed in bfloat16 or wider, within the bound.
No kernel may reach another device: no remote copies, remote signals or barrier semaphores. Data moves between devices by JAX's collectives and lax.ppermute only.
A program may use at most 192 MiB of HBM per device.

v0:
```python
import jax
import jax.numpy as jnp
from jax import lax
from jax.sharding import PartitionSpec as P

BLK = 128
NBLK = 2


def from_root(shard, axis, root):
    mine = lax.axis_index(axis) == root
    return lax.psum(jnp.where(mine, shard, jnp.zeros_like(shard)), axis)


def fetch_split(shrink_store, expand_store, slots):
    per_owner = shrink_store.shape[0]
    pool_count = lax.axis_size("pool")
    me = lax.axis_index("pool")
    shrink_pages = []
    outgoing = []
    owner_list = []
    for slot in slots:
        owner = slot // per_owner
        local = slot % per_owner
        shrink_here = lax.dynamic_index_in_dim(shrink_store, local, 0, keepdims=False)
        shrink_pages.append(from_root(shrink_here, "pool", owner))
        expand_here = lax.dynamic_index_in_dim(expand_store, local, 0, keepdims=False)
        kinds, ranks, units = expand_here.shape
        split_cols = expand_here.reshape(kinds, ranks, pool_count, units // pool_count).transpose(
            2, 0, 1, 3
        )
        mine = (owner == me).astype(split_cols.dtype)
        outgoing.append(split_cols * mine)
        owner_list.append(owner)
    received = lax.all_to_all(
        jnp.stack(outgoing, axis=1), "pool", split_axis=0, concat_axis=0, tiled=True
    )
    expand_pages = []
    for block_index in range(len(slots)):
        from_owner = lax.dynamic_index_in_dim(received, owner_list[block_index], 0, keepdims=False)
        expand_pages.append(from_owner[block_index])
    return (shrink_pages, expand_pages)


def shards(
    tokens,
    gate_up_weight,
    down_weight,
    shrink_store,
    expand_store,
    block_adapter,
    block_live,
    adapter_slot,
):
    highest = lax.Precision.HIGHEST
    width_local = gate_up_weight.shape[0]
    units = gate_up_weight.shape[2]
    total_rows = tokens.shape[1]
    flat_weight = gate_up_weight.reshape(width_local, 2 * units)
    rows_here = total_rows // lax.axis_size("pool")
    positions = lax.axis_index("pool") * rows_here + jnp.arange(rows_here)
    owners = positions // BLK
    results = []
    for decode_step in range(tokens.shape[0]):
        inputs = tokens[decode_step]
        slots = [
            adapter_slot[block_adapter[decode_step, block_index]] for block_index in range(NBLK)
        ]
        shrink_pages, expand_list = fetch_split(shrink_store, expand_store, slots)
        shrunk_list = []
        for block_index in range(NBLK):
            block_rows = inputs[block_index * BLK : (block_index + 1) * BLK]
            shrunk_list.append(
                jnp.einsum(
                    "nd,kdc->knc",
                    block_rows,
                    shrink_pages[block_index],
                    preferred_element_type=jnp.float32,
                )
            )
        shrunk = jnp.concatenate(shrunk_list, axis=1)
        rank_share = lax.psum_scatter(shrunk, "tensor", scatter_dimension=2, tiled=True)
        terms = [
            jnp.einsum(
                "knc,kcf->nkf",
                rank_share[:, block_index * BLK : (block_index + 1) * BLK],
                expand_list[block_index].astype(jnp.float32),
                precision=highest,
            )
            for block_index in range(NBLK)
        ]
        adapted = jnp.concatenate(terms, axis=0)
        partial_sums = (
            jnp.dot(inputs, flat_weight, preferred_element_type=jnp.float32).reshape(
                total_rows, 2, units
            )
            + adapted
        )
        share = lax.psum_scatter(partial_sums, "tensor", scatter_dimension=0, tiled=True)
        hidden_share = (jax.nn.silu(share[:, 0]) * share[:, 1]).astype(jnp.bfloat16)
        hidden = lax.all_gather(hidden_share, "tensor", axis=0, tiled=True)

        def project(first_row, row_count, hidden=hidden):
            return jnp.dot(hidden, down_weight, preferred_element_type=jnp.float32)

        summed = lax.psum_scatter(
            project(jnp.int32(0), rows_here * lax.axis_size("pool")),
            "pool",
            scatter_dimension=0,
            tiled=True,
        )
        live = jnp.sum(
            (owners[:, None] == jnp.arange(NBLK)[None, :]) * block_live[decode_step][None, :],
            axis=1,
        )
        keep = (positions % BLK < live).astype(jnp.float32)
        results.append((summed * keep[:, None]).astype(jnp.bfloat16))
    return jnp.stack(results)


def solution(mesh):
    return jax.shard_map(
        shards,
        mesh=mesh,
        in_specs=(
            P(None, None, "tensor"),
            P("tensor", None, "pool"),
            P("pool", "tensor"),
            P("pool", None, "tensor", None),
            P("pool", None, "tensor", None),
            P(),
            P(),
            P(),
        ),
        out_specs=P(None, "pool", "tensor"),
        check_vma=False,
    )
```

profile of v0, /device:TPU:0, one launch (start us, length us, event | category | flops | bytes accessed | tf_op | source)
XLA Modules:
  0.0 780.8 jit_solution(89996522923451912)
XLA Ops:
  19.7 4.9 broadcast_multiply_fusion.3
  26.0 2.4 copy_bitcast_fusion.2
  28.4 3.6 pad_maximum_fusion
  32.0 8.4 %all-to-all-start = ((bf16[16,2,2,32,1792]{4,3,2,1,0:T(8,128)(2,1)}), bf16[16,2,2,32,1792]{4,3,2,1,0:T(8,128)(2,1)}, u32[]{:S(2)}, u32[]{:S(2)}) async-start(bf16[16,2,2,32,1792]{4,3,2,1,0:T(8,128)(2,1)} %pad_maximum_fusion), calls=%async_computation | async-start | bytes 14680064 | tf_op jit(solution)/shard_map/all_to_all | solution.py:35
  42.9 2.9 copy.24
  46.8 2.4 copy_bitcast_fusion
  49.2 3.6 pad_maximum_fusion.1
  52.8 126.3 %all-to-all-done = bf16[16,2,2,32,1792]{4,3,2,1,0:T(8,128)(2,1)} async-done(((bf16[16,2,2,32,1792]{4,3,2,1,0:T(8,128)(2,1)}), bf16[16,2,2,32,1792]{4,3,2,1,0:T(8,128)(2,1)}, u32[]{:S(2)}, u32[]{:S(2)}) %all-to-all-start) | async-done | bytes 7340064 | tf_op jit(solution)/shard_map/all_to_all | solution.py:35
  179.1 33.6 %all-to-all-start.1 = ((bf16[16,2,2,32,1792]{4,3,2,1,0:T(8,128)(2,1)}), bf16[16,2,2,32,1792]{4,3,2,1,0:T(8,128)(2,1)}, u32[]{:S(2)}, u32[]{:S(2)}) async-start(bf16[16,2,2,32,1792]{4,3,2,1,0:T(8,128)(2,1)} %pad_maximum_fusion.1), calls=%async_computation.4 | async-start | bytes 14680064 | tf_op jit(solution)/shard_map/all_to_all | solution.py:35
  217.7 20.6 %copy.20 = bf16[512,8,2,1792]{3,1,2,0:T(8,128)(2,1)} copy(bf16[512,8,2,1792]{3,2,1,0:T(2,128)(2,1)} %bitcast.148) | data formatting | bytes 58720256
  238.4 37.2 %copy.15 = bf16[3584,4096]{1,0:T(8,128)(2,1)} copy(bf16[3584,4096]{0,1:T(8,128)(2,1)} %bitcast.147) | data formatting | bytes 58720256 | tf_op jit(solution)/shard_map/dot_general | solution.py:94
  276.9 227.6 %all-reduce.3.cloned.1.call-done = (bf16[2,4096,64]{1,2,0:T(8,128)(2,1)}, bf16[2,4096,64]{1,2,0:T(8,128)(2,1)}, bf16[2,4096,64]{1,2,0:T(8,128)(2,1)}, bf16[2,4096,64]{1,2,0:T(8,128)(2,1)}) async-done(((bf16[2,4096,64]{1,2,0:T(8,128)(2,1)}, bf16[2,4096,64]{1,2,0:T(8,128)(2,1)}, bf16[2,4096,64]{1,2,0:T(8,128)(2,1)}, bf16[2,4096,64]{1,2,0:T(8,128)(2,1)}), (bf16[2,4096,64]{1,2,0:T(8,128)(2,1)}, ...) | async-done | bytes 4194320 | tf_op jit(solution)/shard_map/psum | solution.py:12
  504.5 2.1 convolution_bitcast_fusion.6
  513.4 2.5 reduce-scatter.7.cloned.1.call-done
  517.8 3.1 convolution_bitcast_fusion.2
  520.9 15.7 %maximum_add_fusion = f32[256,2,1792]{2,0,1:T(8,128)} fusion(f32[128,2,1792]{2,0,1:T(8,128)} %convolution_bitcast_fusion.2, f32[128,2,1792]{2,0,1:T(8,128)S(1)} %convolution_bitcast_fusion.3, bf16[2,1792,4096]{2,1,0:T(8,128)(2,1)} %bitcast.149, bf16[2,256,4096]{2,1,0:T(8,128)(2,1)} %param.8), kind=kOutput, calls=%fused_computation.2 | convolution fusion | flops 7518027776 | bytes 38797312 | tf_op jit(solution)/shard_map/dot_general | solution.py:94
  540.2 3.1 convolution_bitcast_fusion
  545.3 16.3 %maximum_add_fusion.1 = f32[256,2,1792]{2,0,1:T(8,128)} fusion(f32[128,2,1792]{2,0,1:T(8,128)} %convolution_bitcast_fusion, f32[128,2,1792]{2,0,1:T(8,128)S(1)} %convolution_bitcast_fusion.1, bf16[2,1792,4096]{2,1,0:T(8,128)(2,1)} %bitcast.150, bf16[2,256,4096]{2,1,0:T(8,128)(2,1)} %param.8), kind=kOutput, calls=%fused_computation.3 | convolution fusion | flops 7518027776 | bytes 38797312 | tf_op jit(solution)/shard_map/dot_general | solution.py:94
  563.4 2.7 all_gather.6
  566.1 12.5 %fusion.28 = f32[256,4096]{1,0:T(8,128)} fusion(bf16[256,1792]{1,0:T(8,128)(2,1)S(1)} %all_gather.6, bf16[1792,4096]{1,0:T(8,128)(2,1)} %param.10), kind=kOutput, calls=%fused_computation.78 | convolution fusion | flops 3758096384 | bytes 19791872 | tf_op jit(solution)/shard_map/dot_general | solution.py:104
  580.4 2.5 all_gather.7
  582.8 11.4 %fusion.29 = f32[256,4096]{1,0:T(8,128)} fusion(bf16[256,1792]{1,0:T(8,128)(2,1)S(1)} %all_gather.7, bf16[1792,4096]{1,0:T(8,128)(2,1)} %param.10), kind=kOutput, calls=%fused_computation.79 | convolution fusion | flops 3758096384 | bytes 19791872 | tf_op jit(solution)/shard_map/dot_general | solution.py:104
  595.0 80.1 %reduce-scatter.11.cloned.1.call-done = f32[16,4096]{1,0:T(8,128)} async-done(((f32[256,4096]{1,0:T(8,128)}), f32[16,4096]{1,0:T(8,128)}) %reduce-scatter.11.cloned.1.call-update) | async-done | bytes 262160 | tf_op jit(solution)/shard_map/reduce_scatter | solution.py:106
  676.1 96.1 %reduce-scatter.17.cloned.1.call-done = f32[16,4096]{1,0:T(8,128)} async-done(((f32[256,4096]{1,0:T(8,128)}), f32[16,4096]{1,0:T(8,128)}) %reduce-scatter.17.cloned.1.call-update) | async-done | bytes 262160 | tf_op jit(solution)/shard_map/reduce_scatter | solution.py:106
  (50 shorter events, 25.5 us)
Async XLA Ops:
  32.0 147.1 %all-to-all-start = ((bf16[16,2,2,32,1792]{4,3,2,1,0:T(8,128)(2,1)}), bf16[16,2,2,32,1792]{4,3,2,1,0:T(8,128)(2,1)}, u32[]{:S(2)}, u32[]{:S(2)}) async-start(bf16[16,2,2,32,1792]{4,3,2,1,0:T(8,128)(2,1)} %pad_maximum_fusion), calls=%async_computation | async-start | bytes 14680064 | tf_op jit(solution)/shard_map/all_to_all | solution.py:35
  42.9 3.1 copy-start
  52.8 159.9 %copy-start.1 = (bf16[1,2,4096,64]{2,3,1,0:T(8,128)(2,1)S(1)}, bf16[1,2,4096,64]{2,3,1,0:T(8,128)(2,1)}, u32[]{:S(2)}) copy-start(bf16[1,2,4096,64]{2,3,1,0:T(8,128)(2,1)} %param.11) | copy-start | bytes 3145732
  179.1 361.1 %all-to-all-start.1 = ((bf16[16,2,2,32,1792]{4,3,2,1,0:T(8,128)(2,1)}), bf16[16,2,2,32,1792]{4,3,2,1,0:T(8,128)(2,1)}, u32[]{:S(2)}, u32[]{:S(2)}) async-start(bf16[16,2,2,32,1792]{4,3,2,1,0:T(8,128)(2,1)} %pad_maximum_fusion.1), calls=%async_computation.4 | async-start | bytes 14680064 | tf_op jit(solution)/shard_map/all_to_all | solution.py:35
  212.7 291.8 %all-reduce.3.cloned.1.call-start = ((), (), s32[]{:S(2)}) async-start(), calls=%async_computation.14 | async-start | bytes 8388608 | tf_op jit(solution)/shard_map/psum | solution.py:12
  214.8 301.1 %reduce-scatter.7.cloned.1.call-start = ((), (), s32[]{:S(2)}) async-start(), calls=%async_computation.8 | async-start | bytes 196608 | tf_op jit(solution)/shard_map/reduce_scatter | solution.py:82
  504.5 4.9 copy-start.4
  504.5 6.5 copy-start.3
  509.3 30.9 %reduce-scatter.13.cloned.1.call-start = ((), (), s32[]{:S(2)}) async-start(), calls=%async_computation.11 | async-start | bytes 196608 | tf_op jit(solution)/shard_map/reduce_scatter | solution.py:82
  513.4 48.3 %reduce-scatter.9.cloned.1.call-start = ((), (), s32[]{:S(2)}) async-start(), calls=%async_computation.9 | async-start | bytes 5505024 | tf_op jit(solution)/shard_map/reduce_scatter | solution.py:99
  536.6 42.1 %reduce-scatter.15.cloned.1.call-start = ((), (), s32[]{:S(2)}) async-start(), calls=%async_computation.12 | async-start | bytes 5505024 | tf_op jit(solution)/shard_map/reduce_scatter | solution.py:99
  561.6 113.4 %reduce-scatter.11.cloned.1.call-start = ((), (), s32[]{:S(2)}) async-start(), calls=%async_computation.10 | async-start | bytes 4456448 | tf_op jit(solution)/shard_map/reduce_scatter | solution.py:106
  578.6 193.6 %reduce-scatter.17.cloned.1.call-start = ((), (), s32[]{:S(2)}) async-start(), calls=%async_computation.13 | async-start | bytes 4456448 | tf_op jit(solution)/shard_map/reduce_scatter | solution.py:106
  594.2 0.7 copy-start.2
Sparse Core Ops, SparseCore 0:
  219.6 284.8 all-reduce.2
  509.4 6.4 reduce-scatter.6
  518.2 8.6 reduce-scatter.12
  536.7 12.6 reduce-scatter.8
  561.7 12.6 reduce-scatter.14
  578.7 96.3 reduce-scatter.10
  677.4 94.6 reduce-scatter.16
where the time goes:
time: 783 us; the launch traced here: 781 us
  waiting for transfers between devices  533 us (68%)
  matrix products  73.2 us (9%)
  local copies, waits for them, and re-layouts  71.5 us (9%)
  starting transfers between devices  42.4 us (5%)
  between operations  34 us (4%)
  other arithmetic  21.9 us (3%)
    psum x1, waiting for transfers between devices, from_root(): return lax.psum(jnp.where(mine, shard, jnp.zeros_like(shard)), axis)  228 us
    reduce_scatter x2, waiting for transfers between devices, shards(): lax.psum_scatter(project(jnp.int32(0), rows_here * lax.axis_size('pool'))...  176 us
    all_to_all x2, waiting for transfers between devices, fetch_split(): lax.all_to_all(jnp.stack(outgoing, axis=1), 'pool', split_axis=0, concat_...  126 us
    all_to_all x2, starting transfers between devices, fetch_split(): lax.all_to_all(jnp.stack(outgoing, axis=1), 'pool', split_axis=0, concat_...  41.9 us
    dot_general x1, local copies, waits for them, and re-layouts, shards(): jnp.dot(inputs, flat_weight, preferred_element_type=jnp.float32)  37.2 us
    dot_general x2, matrix products, shards(): jnp.dot(inputs, flat_weight, preferred_element_type=jnp.float32)  31.9 us
    unnamed x15, local copies, waits for them, and re-layouts  26.6 us
    dot_general x2, matrix products, project(): return jnp.dot(hidden, down_weight, preferred_element_type=jnp.float32)  23.8 us
  transfers between devices with their start and end apart: 9, of which 5 were waited for; matrix products, arithmetic and copies ran while one was open for 19% of the time, Pallas kernels for 0%

commit v1 on v0

v1 whole, which is shorter than its diff:
```python
import jax
import jax.numpy as jnp
from jax import lax
from jax.sharding import PartitionSpec as P

BLK = 128
NBLK = 2


def pool_reduce(part, order):
    count = lax.axis_size("pool")
    me = lax.axis_index("pool")
    bits = count.bit_length() - 1
    rows, cols = part.shape
    current = part.reshape((2,) * bits + (rows // count, cols))
    left = list(reversed(range(bits)))
    for bit in order:
        axis = left.index(bit)
        left.remove(bit)
        mine = (me >> bit) & 1
        keep = lax.dynamic_index_in_dim(current, mine, axis, keepdims=False)
        send = lax.dynamic_index_in_dim(current, 1 - mine, axis, keepdims=False)
        got = lax.ppermute(
            send.astype(jnp.bfloat16), "pool", [(i, i ^ (1 << bit)) for i in range(count)]
        )
        current = keep + got.astype(jnp.float32)
    return current


def shards(
    tokens,
    gate_up_weight,
    down_weight,
    shrink_store,
    expand_store,
    block_adapter,
    block_live,
    adapter_slot,
):
    steps, total_rows, width_local = tokens.shape
    units = gate_up_weight.shape[2]
    pool_count = lax.axis_size("pool")
    tensor_count = lax.axis_size("tensor")
    me = lax.axis_index("pool")
    kinds = gate_up_weight.shape[1]
    ranks_local = expand_store.shape[2]
    rank = ranks_local * tensor_count
    units_here = units // tensor_count
    rows_here = total_rows // pool_count
    bits = pool_count.bit_length() - 1
    slots = adapter_slot[block_adapter]

    outgoing = expand_store[0].reshape(kinds, ranks_local, pool_count * tensor_count, units_here)
    outgoing = outgoing.transpose(2, 0, 1, 3)
    second = lax.all_to_all(outgoing, ("pool", "tensor"), split_axis=0, concat_axis=0, tiled=True)
    second = second.reshape(pool_count, tensor_count, kinds, ranks_local, units_here)

    first = jnp.einsum(
        "snd,kdc->snkc", tokens, shrink_store[0], preferred_element_type=jnp.float32
    )
    mine = jnp.repeat((slots == me).astype(jnp.float32), total_rows // NBLK, axis=1)
    shrunk = lax.psum(first * mine[:, :, None, None], ("pool", "tensor"))

    flat_tokens = tokens.reshape(steps * total_rows, width_local)
    grouped = gate_up_weight.reshape(width_local // 8, 8, kinds, units).transpose(0, 2, 1, 3)
    partial_sums = jnp.stack(
        [
            jnp.dot(
                flat_tokens,
                grouped[:, kind].reshape(width_local, units),
                preferred_element_type=jnp.float32,
            )
            for kind in range(kinds)
        ]
    )
    main = lax.psum_scatter(partial_sums, "tensor", scatter_dimension=2, tiled=True)
    main = main.reshape(kinds, steps, NBLK, BLK, units_here)
    shrunk = shrunk.reshape(steps, NBLK, BLK, kinds, rank)
    high = shrunk.astype(jnp.bfloat16)
    low = (shrunk - high.astype(jnp.float32)).astype(jnp.bfloat16)
    shrunk = jnp.concatenate([high, low], axis=4)
    hidden_blocks = []
    for step in range(steps):
        for block in range(NBLK):
            page = lax.dynamic_index_in_dim(second, slots[step, block], 0, keepdims=False)
            page = page.transpose(1, 0, 2, 3).reshape(kinds, rank, units_here)
            gate, up = [
                main[kind, step, block]
                + jnp.dot(
                    shrunk[step, block, :, kind],
                    jnp.concatenate([page[kind], page[kind]], axis=0),
                    preferred_element_type=jnp.float32,
                )
                for kind in range(kinds)
            ]
            hidden_blocks.append((jax.nn.silu(gate) * up).astype(jnp.bfloat16))
    hidden = lax.all_gather(jnp.concatenate(hidden_blocks, axis=0), "tensor", axis=1, tiled=True)

    positions = me * rows_here + jnp.arange(rows_here)
    owners = positions // BLK
    half = down_weight.shape[1] // 2
    orders = [list(range(bits)), [1, 0] + list(range(2, bits))]
    results = []
    for step in range(steps):
        live = jnp.sum(
            (owners[:, None] == jnp.arange(NBLK)[None, :]) * block_live[step][None, :], axis=1
        )
        keep = (positions % BLK < live).astype(jnp.float32)
        pieces = []
        for piece in range(2):
            part = jnp.dot(
                hidden[step * total_rows : (step + 1) * total_rows],
                down_weight[:, piece * half : (piece + 1) * half],
                preferred_element_type=jnp.float32,
            )
            pieces.append(pool_reduce(part, orders[piece]))
        summed = jnp.concatenate(pieces, axis=1)
        results.append((summed * keep[:, None]).astype(jnp.bfloat16))
    return jnp.stack(results)


def solution(mesh):
    return jax.shard_map(
        shards,
        mesh=mesh,
        in_specs=(
            P(None, None, "tensor"),
            P("tensor", None, "pool"),
            P("pool", "tensor"),
            P("pool", None, "tensor", None),
            P("pool", None, "tensor", None),
            P(),
            P(),
            P(),
        ),
        out_specs=P(None, "pool", "tensor"),
        check_vma=False,
    )
```

time: 783 us -> 254 us (0.32)
  waiting for transfers between devices: 533 us -> 117 us
  local copies, waits for them, and re-layouts: 71.5 us -> 31.8 us
  matrix products: 73.2 us -> 46.2 us
  starting transfers between devices: 42.4 us -> 26.4 us
  other arithmetic: 21.9 us -> 8.27 us
  between operations: 34 us -> 23.1 us
    reduce_scatter x6 -> x1, waiting for transfers between devices: 179 us -> 0.03 us  [shards(): lax.psum_scatter(partial_sums, 'tensor', scatter_dimension=2, tiled=True)]
    psum x1, waiting for transfers between devices: 228 us -> 77.6 us  [shards(): shrunk = lax.psum(first * mine[:, :, None, None], ('pool', 'tensor'))]
    all_to_all x2 -> x1, waiting for transfers between devices: 126 us -> 0.01 us  [shards(): lax.all_to_all(outgoing, ('pool', 'tensor'), split_axis=0, concat_axis=0,...]
    dot_general x1 -> x0, local copies, waits for them, and re-layouts: 37.2 us -> none  [shards(): jnp.dot(inputs, flat_weight, preferred_element_type=jnp.float32)]
    all_to_all x2 -> x1, starting transfers between devices: 41.9 us -> 7.42 us  [shards(): lax.all_to_all(outgoing, ('pool', 'tensor'), split_axis=0, concat_axis=0,...]
    ppermute x0 -> x16, waiting for transfers between devices: none -> 31 us  [pool_reduce(): lax.ppermute(send.astype(jnp.bfloat16), 'pool', [(i, i ^ 1 << bit) for i...]
    dot_general x12 -> x15, matrix products: 73.2 us -> 46.2 us  [the longest x2 22.2 us: shards(): jnp.dot(flat_tokens, grouped[:, kind].reshape(width_local, units), prefer...]
    ppermute x0 -> x16, starting transfers between devices: none -> 18.8 us  [pool_reduce(): lax.ppermute(send.astype(jnp.bfloat16), 'pool', [(i, i ^ 1 << bit) for i...]
  transfers between devices with their start and end apart: 9 -> 20, of which waited for: 5 -> 12; matrix products, arithmetic and copies ran while one was open for 19% -> 26% of each run, Pallas kernels for 0% -> 0%
where the time goes in v1:
time: 254 us; the launch traced here: 253 us
  waiting for transfers between devices  117 us (46%)
  matrix products  46.2 us (18%)
  local copies, waits for them, and re-layouts  31.8 us (13%)
  starting transfers between devices  26.4 us (10%)
  between operations  23.1 us (9%)
  other arithmetic  8.27 us (3%)
    psum x1, waiting for transfers between devices, shards(): shrunk = lax.psum(first * mine[:, :, None, None], ('pool', 'tensor'))  77.6 us
    ppermute x16, waiting for transfers between devices, pool_reduce(): lax.ppermute(send.astype(jnp.bfloat16), 'pool', [(i, i ^ 1 << bit) for i...  31 us
    unnamed x24, local copies, waits for them, and re-layouts  23.1 us
    dot_general x2, matrix products, shards(): jnp.dot(flat_tokens, grouped[:, kind].reshape(width_local, units), prefer...  22.2 us
    ppermute x16, starting transfers between devices, pool_reduce(): lax.ppermute(send.astype(jnp.bfloat16), 'pool', [(i, i ^ 1 << bit) for i...  18.8 us
    dot_general x4, matrix products, shards(): jnp.dot(hidden[step * total_rows:(step + 1) * total_rows], down_weight[:,...  14.8 us
    all_gather x1, waiting for transfers between devices, shards(): lax.all_gather(jnp.concatenate(hidden_blocks, axis=0), 'tensor', axis=1,...  8.73 us
    all_to_all x1, starting transfers between devices, shards(): lax.all_to_all(outgoing, ('pool', 'tensor'), split_axis=0, concat_axis=0,...  7.42 us
  transfers between devices with their start and end apart: 20, of which 12 were waited for; matrix products, arithmetic and copies ran while one was open for 26% of the time, Pallas kernels for 0%

profile of v1, /device:TPU:0, one launch (start us, length us, event | category | flops | bytes accessed | tf_op | source)
XLA Modules:
  0.0 253.2 jit_solution(9959674933152894542)
XLA Ops:
  9.7 3.7 %fusion.22 = f32[2,256,2,64]{1,3,2,0:T(8,128)S(1)} fusion(bf16[2,256,4096]{2,1,0:T(8,128)(2,1)} %param.8, bf16[1,2,4096,64]{2,3,1,0:T(8,128)(2,1)S(1)} %copy-done, f32[2,256]{1,0:T(2,128)S(1)} %bitcast.253), kind=kOutput, calls=%fused_computation.36 | convolution fusion | flops 536936448 | bytes 5507072 | tf_op jit(solution)/shard_map/snd,kdc->snkc/dot_general | solution.py:58
  14.6 20.3 %copy.95 = bf16[4096,2,1792]{2,0,1:T(8,128)(2,1)} copy(bf16[4096,2,1792]{2,1,0:T(2,128)(2,1)} %param.9) | data formatting | bytes 58720256 | tf_op args[1]
  35.0 11.8 %fusion.13 = f32[1,512,1792]{2,1,0:T(8,128)S(1)} fusion(bf16[512,4096]{1,0:T(8,128)(2,1)} %bitcast.256, bf16[512,2,8,1792]{3,2,0,1:T(8,128)(2,1)} %bitcast.225), kind=kOutput, calls=%fused_computation.19 | convolution fusion | flops 7516192768 | bytes 22544384 | tf_op jit(solution)/shard_map/dot_general | solution.py:68
  46.8 10.4 %fusion.12 = f32[1,512,1792]{2,1,0:T(8,128)S(1)} fusion(bf16[512,4096]{1,0:T(8,128)(2,1)S(1)} %bitcast.257, bf16[512,2,8,1792]{3,2,0,1:T(8,128)(2,1)} %bitcast.226), kind=kOutput, calls=%fused_computation.18 | convolution fusion | flops 7516192768 | bytes 22544384 | tf_op jit(solution)/shard_map/dot_general | solution.py:68
  57.2 3.4 %pad_maximum_fusion = f32[2,512,1792]{2,1,0:T(8,128)} fusion(f32[1,512,1792]{2,1,0:T(8,128)S(1)} %fusion.13, f32[1,512,1792]{2,1,0:T(8,128)S(1)} %fusion.12), kind=kLoop, calls=%fused_computation.6 | loop fusion | flops 1835008 | bytes 14680064 | tf_op jit(solution)/shard_map/stack | solution.py:66
  60.6 2.6 %copy.76 = bf16[8,8,32,896]{3,2,1,0:T(8,128)(2,1)S(1)} copy(bf16[8,8,32,896]{3,1,2,0:T(8,128)(2,1)} %bitcast.228) | data formatting | bytes 7340032
  63.6 3.1 %copy.61 = bf16[32,2,32,896]{3,2,1,0:T(8,128)(2,1)} copy(bf16[32,2,32,896]{3,0,2,1:T(8,128)(2,1)S(1)} %bitcast_bitcast_fusion) | data formatting | bytes 7340032 | tf_op jit(solution)/shard_map/transpose | solution.py:54
  66.7 7.4 %all-to-all-start = ((bf16[32,2,32,896]{3,2,1,0:T(8,128)(2,1)}), bf16[32,2,32,896]{3,2,1,0:T(8,128)(2,1)}, u32[]{:S(2)}, u32[]{:S(2)}) async-start(bf16[32,2,32,896]{3,2,1,0:T(8,128)(2,1)} %copy.61), calls=%async_computation.1 | async-start | bytes 7340032 | tf_op jit(solution)/shard_map/all_to_all | solution.py:55
  82.7 77.6 %all-reduce.2.cloned.1.call-done = f32[2,2,128,2,64]{4,2,3,1,0:T(8,128)} async-done(((f32[2,2,128,2,64]{4,2,3,1,0:T(8,128)}), f32[2,2,128,2,64]{4,2,3,1,0:T(8,128)}) %all-reduce.2.cloned.1.call-update) | async-done | bytes 262160 | tf_op jit(solution)/shard_map/psum | solution.py:62
  169.9 8.7 %all-gather.2.cloned.1.call-done = bf16[512,1792]{1,0:T(8,128)(2,1)} async-done(((bf16[512,896]{1,0:T(8,128)(2,1)}), bf16[512,1792]{1,0:T(8,128)(2,1)}) %all-gather.2.cloned.1.call-update) | async-done | bytes 1835024 | tf_op jit(solution)/shard_map/all_gather | solution.py:97
  178.6 5.6 %fusion.2 = f32[256,2048]{1,0:T(8,128)S(1)} fusion(bf16[1792,4096]{1,0:T(8,128)(2,1)} %param.10, bf16[512,1792]{1,0:T(8,128)(2,1)} %all-gather.2.cloned.1.call-done), kind=kOutput, calls=%fused_computation.7 | convolution fusion | flops 1879048192 | bytes 10354688 | tf_op jit(solution)/shard_map/dot_general | solution.py:111
  186.1 5.1 %fusion.6 = f32[256,2048]{1,0:T(8,128)S(1)} fusion(bf16[1792,4096]{1,0:T(8,128)(2,1)} %param.10, bf16[512,1792]{1,0:T(8,128)(2,1)S(1)} %copy-done.5), kind=kOutput, calls=%fused_computation.11 | convolution fusion | flops 1879048192 | bytes 10354688 | tf_op jit(solution)/shard_map/dot_general | solution.py:111
  193.1 2.1 fusion.4
  195.9 2.1 fusion.8
  199.1 1.9 collective-permute-start.13
  201.1 5.1 %collective-permute-done.8 = bf16[2,2,2,16,2048]{4,3,0,1,2:T(8,128)(2,1)S(1)} collective-permute-done((bf16[2,2,2,16,2048]{4,3,0,1,2:T(8,128)(2,1)S(1)}, bf16[2,2,2,16,2048]{4,3,0,1,2:T(8,128)(2,1)S(1)}, u32[]{:S(2)}, u32[]{:S(2)}) %collective-permute-start.8) | collective-permute-done | bytes 524320 | tf_op jit(solution)/shard_map/ppermute | solution.py:23
  206.8 3.4 %collective-permute-done.4 = bf16[2,2,2,16,2048]{4,3,0,1,2:T(8,128)(2,1)S(1)} collective-permute-done((bf16[2,2,2,16,2048]{4,3,0,1,2:T(8,128)(2,1)S(1)}, bf16[2,2,2,16,2048]{4,3,0,1,2:T(8,128)(2,1)S(1)}, u32[]{:S(2)}, u32[]{:S(2)}) %collective-permute-start.4) | collective-permute-done | bytes 524320 | tf_op jit(solution)/shard_map/ppermute | solution.py:23
  210.4 1.9 collective-permute-start.5
  212.3 5.1 %collective-permute-done = bf16[2,2,2,16,2048]{4,3,0,1,2:T(8,128)(2,1)S(1)} collective-permute-done((bf16[2,2,2,16,2048]{4,3,0,1,2:T(8,128)(2,1)S(1)}, bf16[2,2,2,16,2048]{4,3,0,1,2:T(8,128)(2,1)S(1)}, u32[]{:S(2)}, u32[]{:S(2)}) %collective-permute-start) | collective-permute-done | bytes 524320 | tf_op jit(solution)/shard_map/ppermute | solution.py:23
  218.0 5.0 %collective-permute-done.13 = bf16[2,2,16,2048]{3,2,0,1:T(8,128)(2,1)S(1)} collective-permute-done((bf16[2,2,16,2048]{3,2,0,1:T(8,128)(2,1)S(1)}, bf16[2,2,16,2048]{3,2,0,1:T(8,128)(2,1)S(1)}, u32[]{:S(2)}, u32[]{:S(2)}) %collective-permute-start.13) | collective-permute-done | bytes 262176 | tf_op jit(solution)/shard_map/ppermute | solution.py:23
  225.3 2.6 %collective-permute-done.5 = bf16[2,2,16,2048]{3,2,0,1:T(8,128)(2,1)S(1)} collective-permute-done((bf16[2,2,16,2048]{3,2,0,1:T(8,128)(2,1)S(1)}, bf16[2,2,16,2048]{3,2,0,1:T(8,128)(2,1)S(1)}, u32[]{:S(2)}, u32[]{:S(2)}) %collective-permute-start.5) | collective-permute-done | bytes 262176 | tf_op jit(solution)/shard_map/ppermute | solution.py:23
  230.4 2.7 %collective-permute-start.15 = (bf16[16,2048]{1,0:T(8,128)(2,1)S(1)}, bf16[16,2048]{1,0:T(8,128)(2,1)S(1)}, u32[]{:S(2)}, u32[]{:S(2)}) collective-permute-start(bf16[16,2048]{1,0:T(8,128)(2,1)S(1)} %fusion.75), channel_id=1, source_target_pairs={{0,16},{2,18},{4,20},{6,22},{8,24},{10,26},{12,28},{14,30},{16,0},... | collective-permute-start | bytes 196616 | tf_op jit(solution)/shard_map/ppermute | solution.py:23
  233.5 3.6 %collective-permute-done.6 = bf16[2,16,2048]{2,1,0:T(8,128)(2,1)S(1)} collective-permute-done((bf16[2,16,2048]{2,1,0:T(8,128)(2,1)S(1)}, bf16[2,16,2048]{2,1,0:T(8,128)(2,1)S(1)}, u32[]{:S(2)}, u32[]{:S(2)}) %collective-permute-start.6) | collective-permute-done | bytes 131104 | tf_op jit(solution)/shard_map/ppermute | solution.py:23
  240.5 3.8 %collective-permute-done.7 = bf16[16,2048]{1,0:T(8,128)(2,1)S(1)} collective-permute-done((bf16[16,2048]{1,0:T(8,128)(2,1)S(1)}, bf16[16,2048]{1,0:T(8,128)(2,1)S(1)}, u32[]{:S(2)}, u32[]{:S(2)}) %collective-permute-start.7) | collective-permute-done | bytes 65568 | tf_op jit(solution)/shard_map/ppermute | solution.py:23
  (115 shorter events, 31.2 us)
Async XLA Ops:
  7.4 152.9 %all-reduce.2.cloned.1.call-start = ((), (), s32[]{:S(2)}) async-start(), calls=%async_computation.3 | async-start | bytes 1048576 | tf_op jit(solution)/shard_map/psum | solution.py:62
  14.6 148.5 %reduce-scatter.2.cloned.1.call-start = ((), (), s32[]{:S(2)}) async-start(), calls=%async_computation.2 | async-start | bytes 11010048 | tf_op jit(solution)/shard_map/reduce_scatter | solution.py:76
  35.0 11.8 %copy-start.4 = (bf16[2,256,4096]{2,1,0:T(8,128)(2,1)S(1)}, bf16[2,256,4096]{2,1,0:T(8,128)(2,1)}, u32[]{:S(2)}) copy-start(bf16[2,256,4096]{2,1,0:T(8,128)(2,1)} %param.8) | copy-start | bytes 12582916
  66.7 94.9 %all-to-all-start = ((bf16[32,2,32,896]{3,2,1,0:T(8,128)(2,1)}), bf16[32,2,32,896]{3,2,1,0:T(8,128)(2,1)}, u32[]{:S(2)}, u32[]{:S(2)}) async-start(bf16[32,2,32,896]{3,2,1,0:T(8,128)(2,1)} %copy.61), calls=%async_computation.1 | async-start | bytes 7340032 | tf_op jit(solution)/shard_map/all_to_all | solution.py:55
  74.1 104.5 %all-gather.2.cloned.1.call-start = ((), (), s32[]{:S(2)}) async-start(), calls=%async_computation.4 | async-start | bytes 2752512 | tf_op jit(solution)/shard_map/all_gather | solution.py:97
  178.6 14.5 %slice-start = ((s8[14680064]{0:T(1024)(128)(4,1)}), s8[4194304]{0:T(1024)(128)(4,1)S(1)}, s32[]{:S(2)}) async-start(s8[14680064]{0:T(1024)(128)(4,1)} %bitcast.254), calls=%async_computation.5 | async-start | bytes 8388608
  178.6 14.5 %slice-start.1 = ((s8[14680064]{0:T(1024)(128)(4,1)}), s8[4194304]{0:T(1024)(128)(4,1)S(1)}, s32[]{:S(2)}) async-start(s8[14680064]{0:T(1024)(128)(4,1)} %bitcast.254), calls=%async_computation.6 | async-start | bytes 8388608
  184.3 14.7 %collective-permute-start.12 = (bf16[2,2,2,16,2048]{4,3,0,1,2:T(8,128)(2,1)S(1)}, bf16[2,2,2,16,2048]{4,3,0,1,2:T(8,128)(2,1)S(1)}, u32[]{:S(2)}, u32[]{:S(2)}) collective-permute-start(bf16[2,2,2,16,2048]{4,3,0,1,2:T(8,128)(2,1)S(1)} %fusion.33), channel_id=1, source_target_pairs={{0,4},{2,6},{4,0},{6,2},{8,12},{10,14},{12,8},{14,10},{16,20},{18,... | collective-permute-start | bytes 1572872 | tf_op jit(solution)/shard_map/ppermute | solution.py:23
  191.3 14.8 %collective-permute-start.8 = (bf16[2,2,2,16,2048]{4,3,0,1,2:T(8,128)(2,1)S(1)}, bf16[2,2,2,16,2048]{4,3,0,1,2:T(8,128)(2,1)S(1)}, u32[]{:S(2)}, u32[]{:S(2)}) collective-permute-start(bf16[2,2,2,16,2048]{4,3,0,1,2:T(8,128)(2,1)S(1)} %fusion.32), channel_id=1, source_target_pairs={{0,2},{2,0},{4,6},{6,4},{8,10},{10,8},{12,14},{14,12},{16,18},{18,... | collective-permute-start | bytes 1572872 | tf_op jit(solution)/shard_map/ppermute | solution.py:23
  195.3 15.0 %collective-permute-start.4 = (bf16[2,2,2,16,2048]{4,3,0,1,2:T(8,128)(2,1)S(1)}, bf16[2,2,2,16,2048]{4,3,0,1,2:T(8,128)(2,1)S(1)}, u32[]{:S(2)}, u32[]{:S(2)}) collective-permute-start(bf16[2,2,2,16,2048]{4,3,0,1,2:T(8,128)(2,1)S(1)} %fusion.31), channel_id=1, source_target_pairs={{0,4},{2,6},{4,0},{6,2},{8,12},{10,14},{12,8},{14,10},{16,20},{18,... | collective-permute-start | bytes 1572872 | tf_op jit(solution)/shard_map/ppermute | solution.py:23
  198.0 19.3 %collective-permute-start = (bf16[2,2,2,16,2048]{4,3,0,1,2:T(8,128)(2,1)S(1)}, bf16[2,2,2,16,2048]{4,3,0,1,2:T(8,128)(2,1)S(1)}, u32[]{:S(2)}, u32[]{:S(2)}) collective-permute-start(bf16[2,2,2,16,2048]{4,3,0,1,2:T(8,128)(2,1)S(1)} %fusion.30), channel_id=1, source_target_pairs={{0,2},{2,0},{4,6},{6,4},{8,10},{10,8},{12,14},{14,12},{16,18},{18,... | collective-permute-start | bytes 1572872 | tf_op jit(solution)/shard_map/ppermute | solution.py:23
  199.1 23.9 %collective-permute-start.13 = (bf16[2,2,16,2048]{3,2,0,1:T(8,128)(2,1)S(1)}, bf16[2,2,16,2048]{3,2,0,1:T(8,128)(2,1)S(1)}, u32[]{:S(2)}, u32[]{:S(2)}) collective-permute-start(bf16[2,2,16,2048]{3,2,0,1:T(8,128)(2,1)S(1)} %fusion.37), channel_id=1, source_target_pairs={{0,2},{2,0},{4,6},{6,4},{8,10},{10,8},{12,14},{14,12},{16,18},{18,... | collective-permute-start | bytes 786440 | tf_op jit(solution)/shard_map/ppermute | solution.py:23
  206.3 18.6 %collective-permute-start.9 = (bf16[2,2,16,2048]{3,2,0,1:T(8,128)(2,1)S(1)}, bf16[2,2,16,2048]{3,2,0,1:T(8,128)(2,1)S(1)}, u32[]{:S(2)}, u32[]{:S(2)}) collective-permute-start(bf16[2,2,16,2048]{3,2,0,1:T(8,128)(2,1)S(1)} %fusion.36), channel_id=1, source_target_pairs={{0,4},{2,6},{4,0},{6,2},{8,12},{10,14},{12,8},{14,10},{16,20},{18,... | collective-permute-start | bytes 786440 | tf_op jit(solution)/shard_map/ppermute | solution.py:23
  210.4 17.6 %collective-permute-start.5 = (bf16[2,2,16,2048]{3,2,0,1:T(8,128)(2,1)S(1)}, bf16[2,2,16,2048]{3,2,0,1:T(8,128)(2,1)S(1)}, u32[]{:S(2)}, u32[]{:S(2)}) collective-permute-start(bf16[2,2,16,2048]{3,2,0,1:T(8,128)(2,1)S(1)} %fusion.35), channel_id=1, source_target_pairs={{0,2},{2,0},{4,6},{6,4},{8,10},{10,8},{12,14},{14,12},{16,18},{18,... | collective-permute-start | bytes 786440 | tf_op jit(solution)/shard_map/ppermute | solution.py:23
  217.5 12.3 %collective-permute-start.1 = (bf16[2,2,16,2048]{3,2,0,1:T(8,128)(2,1)S(1)}, bf16[2,2,16,2048]{3,2,0,1:T(8,128)(2,1)S(1)}, u32[]{:S(2)}, u32[]{:S(2)}) collective-permute-start(bf16[2,2,16,2048]{3,2,0,1:T(8,128)(2,1)S(1)} %fusion.34), channel_id=1, source_target_pairs={{0,4},{2,6},{4,0},{6,2},{8,12},{10,14},{12,8},{14,10},{16,20},{18,... | collective-permute-start | bytes 786440 | tf_op jit(solution)/shard_map/ppermute | solution.py:23
  223.1 7.2 %collective-permute-start.14 = (bf16[2,16,2048]{2,1,0:T(8,128)(2,1)S(1)}, bf16[2,16,2048]{2,1,0:T(8,128)(2,1)S(1)}, u32[]{:S(2)}, u32[]{:S(2)}) collective-permute-start(bf16[2,16,2048]{2,1,0:T(8,128)(2,1)S(1)} %fusion.67), channel_id=1, source_target_pairs={{0,8},{2,10},{4,12},{6,14},{8,0},{10,2},{12,4},{14,6},{16,24},{18,... | collective-permute-start | bytes 393224 | tf_op jit(solution)/shard_map/ppermute | solution.py:23
  224.9 8.2 %collective-permute-start.10 = (bf16[2,16,2048]{2,1,0:T(8,128)(2,1)S(1)}, bf16[2,16,2048]{2,1,0:T(8,128)(2,1)S(1)}, u32[]{:S(2)}, u32[]{:S(2)}) collective-permute-start(bf16[2,16,2048]{2,1,0:T(8,128)(2,1)S(1)} %fusion.66), channel_id=1, source_target_pairs={{0,8},{2,10},{4,12},{6,14},{8,0},{10,2},{12,4},{14,6},{16,24},{18,... | collective-permute-start | bytes 393224 | tf_op jit(solution)/shard_map/ppermute | solution.py:23
  228.0 17.8 %copy-start.1 = (bf16[1,2,4096,64]{2,3,1,0:T(8,128)(2,1)S(1)}, bf16[1,2,4096,64]{2,3,1,0:T(8,128)(2,1)}, u32[]{:S(2)}) copy-start(bf16[1,2,4096,64]{2,3,1,0:T(8,128)(2,1)} %param.11) | copy-start | bytes 3145732
  228.0 9.0 %collective-permute-start.6 = (bf16[2,16,2048]{2,1,0:T(8,128)(2,1)S(1)}, bf16[2,16,2048]{2,1,0:T(8,128)(2,1)S(1)}, u32[]{:S(2)}, u32[]{:S(2)}) collective-permute-start(bf16[2,16,2048]{2,1,0:T(8,128)(2,1)S(1)} %fusion.65), channel_id=1, source_target_pairs={{0,8},{2,10},{4,12},{6,14},{8,0},{10,2},{12,4},{14,6},{16,24},{18,... | collective-permute-start | bytes 393224 | tf_op jit(solution)/shard_map/ppermute | solution.py:23
  230.0 9.6 %collective-permute-start.2 = (bf16[2,16,2048]{2,1,0:T(8,128)(2,1)S(1)}, bf16[2,16,2048]{2,1,0:T(8,128)(2,1)S(1)}, u32[]{:S(2)}, u32[]{:S(2)}) collective-permute-start(bf16[2,16,2048]{2,1,0:T(8,128)(2,1)S(1)} %fusion.64), channel_id=1, source_target_pairs={{0,8},{2,10},{4,12},{6,14},{8,0},{10,2},{12,4},{14,6},{16,24},{18,... | collective-permute-start | bytes 393224 | tf_op jit(solution)/shard_map/ppermute | solution.py:23
  230.4 10.0 %collective-permute-start.15 = (bf16[16,2048]{1,0:T(8,128)(2,1)S(1)}, bf16[16,2048]{1,0:T(8,128)(2,1)S(1)}, u32[]{:S(2)}, u32[]{:S(2)}) collective-permute-start(bf16[16,2048]{1,0:T(8,128)(2,1)S(1)} %fusion.75), channel_id=1, source_target_pairs={{0,16},{2,18},{4,20},{6,22},{8,24},{10,26},{12,28},{14,30},{16,0},... | collective-permute-start | bytes 196616 | tf_op jit(solution)/shard_map/ppermute | solution.py:23
  233.2 7.2 %collective-permute-start.11 = (bf16[16,2048]{1,0:T(8,128)(2,1)S(1)}, bf16[16,2048]{1,0:T(8,128)(2,1)S(1)}, u32[]{:S(2)}, u32[]{:S(2)}) collective-permute-start(bf16[16,2048]{1,0:T(8,128)(2,1)S(1)} %fusion.74), channel_id=1, source_target_pairs={{0,16},{2,18},{4,20},{6,22},{8,24},{10,26},{12,28},{14,30},{16,0},... | collective-permute-start | bytes 196616 | tf_op jit(solution)/shard_map/ppermute | solution.py:23
  237.1 7.2 %collective-permute-start.7 = (bf16[16,2048]{1,0:T(8,128)(2,1)S(1)}, bf16[16,2048]{1,0:T(8,128)(2,1)S(1)}, u32[]{:S(2)}, u32[]{:S(2)}) collective-permute-start(bf16[16,2048]{1,0:T(8,128)(2,1)S(1)} %fusion.73), channel_id=1, source_target_pairs={{0,16},{2,18},{4,20},{6,22},{8,24},{10,26},{12,28},{14,30},{16,0},... | collective-permute-start | bytes 196616 | tf_op jit(solution)/shard_map/ppermute | solution.py:23
  239.6 5.4 %collective-permute-start.3 = (bf16[16,2048]{1,0:T(8,128)(2,1)S(1)}, bf16[16,2048]{1,0:T(8,128)(2,1)S(1)}, u32[]{:S(2)}, u32[]{:S(2)}) collective-permute-start(bf16[16,2048]{1,0:T(8,128)(2,1)S(1)} %fusion.72), channel_id=1, source_target_pairs={{0,16},{2,18},{4,20},{6,22},{8,24},{10,26},{12,28},{14,30},{16,0},... | collective-permute-start | bytes 196616 | tf_op jit(solution)/shard_map/ppermute | solution.py:23
  (6 other events, 33.2 us)
Sparse Core Ops, SparseCore 0:
  14.7 145.5 all-reduce.1
Sparse Core Ops, SparseCore 1:
  60.7 18.5 reduce-scatter.1
  169.8 8.7 all-gather.1

commit v2 on v1

v2 whole, which is shorter than its diff:
```python
import jax
import jax.numpy as jnp
from jax import lax
from jax.sharding import PartitionSpec as P

BLK = 128
NBLK = 2


def bit_pairs(axis_name, bit):
    return [(i, i ^ (1 << bit)) for i in range(lax.axis_size(axis_name))]


def halve(array, axis_name, bit, axis, wire=None):
    mine = (lax.axis_index(axis_name) >> bit) & 1
    keep = lax.dynamic_index_in_dim(array, mine, axis, keepdims=False)
    send = lax.dynamic_index_in_dim(array, 1 - mine, axis, keepdims=False)
    if wire is not None:
        send = send.astype(wire)
    return keep, send


def swap(array, axis_name, bit):
    return lax.ppermute(array, axis_name, bit_pairs(axis_name, bit))


def bits_of(axis_name):
    return lax.axis_size(axis_name).bit_length() - 1


def scatter_sum(array, axis_name, axis):
    count = bits_of(axis_name)
    shape = array.shape
    length = shape[axis] >> count
    current = array.reshape(shape[:axis] + (2,) * count + (length,) + shape[axis + 1 :])
    for bit in reversed(range(count)):
        keep, send = halve(current, axis_name, bit, axis)
        current = keep + swap(send, axis_name, bit)
    return current


def gather(array, axis_name, axis):
    for bit in range(bits_of(axis_name)):
        mine = (lax.axis_index(axis_name) >> bit) & 1
        got = swap(array, axis_name, bit)
        array = jnp.where(
            mine == 0,
            jnp.concatenate([array, got], axis=axis),
            jnp.concatenate([got, array], axis=axis),
        )
    return array


def sum_all(array, axis_name):
    for bit in range(bits_of(axis_name)):
        array = array + swap(array, axis_name, bit)
    return array


PLANE_BITS = 2
ROUND = 2


def after(array, arrived):
    return lax.optimization_barrier((array, arrived))[0]


def plane_pages(store, arrived, history):
    kinds, ranks, count, cols = store.shape
    width = min(PLANE_BITS, bits_of("pool"))
    held = []
    orders = []
    for kind in range(kinds):
        orders.append([(kind + turn) % width for turn in range(width)])
        held.append({0: store[kind].reshape((ranks, count >> width) + (2,) * width + (cols,))})
    left = [list(reversed(range(width))) for _ in range(kinds)]
    for turn in range(width):
        sends = []
        for kind in range(kinds):
            bit = orders[kind][turn]
            axis = 2 + left[kind].index(bit)
            left[kind].remove(bit)
            split = {place: halve(page, "pool", bit, axis) for place, page in held[kind].items()}
            held[kind] = {place: keep for place, (keep, _) in split.items()}
            sends.append(jnp.stack([send for _, send in split.values()]))
        if arrived is not None and turn == 0:
            sends = after(sends, arrived)
        arrived = []
        for kind in range(kinds):
            bit = orders[kind][turn]
            got = swap(sends[kind], "pool", bit)
            arrived.append(got)
            for row, place in enumerate(list(held[kind])):
                held[kind][place | (1 << bit)] = got[row]
        history.append(arrived)
    pages = [
        [held[kind][place] for kind in range(kinds)] for place in range(1 << width)
    ]
    return pages, arrived


def plane_exchange(pages, chosen):
    me = lax.axis_index("pool")
    width = min(PLANE_BITS, bits_of("pool"))
    planes = lax.axis_size("pool") >> width
    plane = me >> width
    out = []
    for apart in range(planes):
        target = plane ^ apart
        columns = [
            [lax.dynamic_index_in_dim(page, target, 1, keepdims=False) for page in kinds_of]
            for kinds_of in pages
        ]
        picked = jnp.stack(
            [
                jnp.stack(
                    [
                        lax.select_n(choice, *[one[kind] for one in columns])
                        for kind in range(len(pages[0]))
                    ]
                )
                for choice in chosen
            ]
        )
        if apart:
            pairs = [(i, i ^ (apart << width)) for i in range(lax.axis_size("pool"))]
            picked = lax.ppermute(picked, "pool", pairs)
        out.append(picked)
    return out


def shards(
    tokens,
    gate_up_weight,
    down_weight,
    shrink_store,
    expand_store,
    block_adapter,
    block_live,
    adapter_slot,
):
    steps, total_rows, width_local = tokens.shape
    units = gate_up_weight.shape[2]
    pool_count = lax.axis_size("pool")
    tensor_count = lax.axis_size("tensor")
    me = lax.axis_index("pool")
    core = lax.axis_index("tensor")
    kinds = gate_up_weight.shape[1]
    ranks_local = expand_store.shape[2]
    rank = ranks_local * tensor_count
    units_here = units // tensor_count
    rows_here = total_rows // pool_count
    slots = adapter_slot[block_adapter]

    width = min(PLANE_BITS, bits_of("pool"))
    plane_size = 1 << width
    needed = jnp.any(
        slots.reshape(-1)[:, None] == jnp.arange(pool_count)[None, :], axis=0
    ).reshape(-1, plane_size)
    order = jnp.cumsum(needed.astype(jnp.int32), axis=1) - 1
    mine_needed = lax.dynamic_index_in_dim(needed, me >> width, 0, keepdims=False)
    mine_order = lax.dynamic_index_in_dim(order, me >> width, 0, keepdims=False)
    place = me & (plane_size - 1)

    def choice(number):
        hit = mine_needed & (mine_order == number)
        return jnp.sum(jnp.where(hit, jnp.arange(plane_size) ^ place, 0)).astype(jnp.int32)

    store = expand_store[0].reshape(kinds, ranks_local, pool_count, units)
    half_ranks = ranks_local // 2
    arrived = None
    page_sets = []
    history = []
    for part in range(2):
        pages, arrived = plane_pages(
            store[:, part * half_ranks : (part + 1) * half_ranks], arrived, history
        )
        page_sets.append(pages)
    block_number = order.reshape(-1)[slots]
    block_apart = (slots >> width) ^ (me >> width)

    def exchange(first_number):
        chosen = [choice(first_number + m) for m in range(ROUND)]
        sets = [plane_exchange(pages, chosen) for pages in page_sets]
        arrays = [
            jnp.concatenate([one[apart] for one in sets], axis=2) for apart in range(len(sets[0]))
        ]
        everything = jnp.concatenate(arrays, axis=0)
        found = [
            lax.dynamic_index_in_dim(
                everything,
                block_apart[step, block] * ROUND
                + jnp.clip(block_number[step, block] - first_number, 0, ROUND - 1),
                0,
                keepdims=False,
            )
            for step in range(steps)
            for block in range(NBLK)
        ]
        return jnp.stack(found)

    found = exchange(0)
    first = jnp.einsum(
        "snd,kdc->snkc", tokens, shrink_store[0], preferred_element_type=jnp.float32
    )
    mine = jnp.repeat((slots == me).astype(jnp.float32), total_rows // NBLK, axis=1)
    first = first * mine[:, :, None, None]
    first = first.reshape(steps * total_rows, kinds * rank)
    shrunk = gather(sum_all(scatter_sum(first, "tensor", 0), "pool"), "tensor", 0)
    high = shrunk.astype(jnp.bfloat16)
    low = (shrunk - high.astype(jnp.float32)).astype(jnp.bfloat16)

    flat_tokens = tokens.reshape(steps * total_rows, width_local)

    weights = after(gate_up_weight, history[width - 1])
    weights = lax.optimization_barrier(jnp.transpose(weights, (1, 0, 2)))
    main = []
    for kind in range(kinds):
        flat_tokens = after(flat_tokens, history[min(width + kind, len(history) - 1)])
        product = lax.optimization_barrier(
            jnp.dot(flat_tokens, weights[kind], preferred_element_type=jnp.float32)
        )
        if tensor_count == 2:
            low_share, high_share = product[:, :units_here], product[:, units_here:]
            sent = swap(jnp.where(core == 0, high_share, low_share), "tensor", 0)
            main.append(jnp.where(core == 0, low_share, high_share) + sent)
        else:
            main.append(scatter_sum(product, "tensor", 1))

    found, main, high, low = lax.optimization_barrier((found, main, high, low))
    if plane_size > ROUND:
        later = (block_number >= ROUND).reshape(-1)

        def more(found):
            return jnp.where(later[:, None, None, None], exchange(ROUND), found)

        found = lax.cond(jnp.any(later), more, lambda found: found, found)
    found = found.reshape(steps, NBLK, kinds, ranks_local, tensor_count, units_here)

    bits = bits_of("pool")
    positions = me * rows_here + jnp.arange(rows_here)
    owners = positions // BLK
    half = down_weight.shape[1] // 2
    orders = [list(range(bits)), [1, 0] + list(range(2, bits))]
    sums = []
    arrived = None
    for step in range(steps):
        second = found[step]
        tensor_bits = bits_of("tensor")
        second = second.reshape(
            (NBLK, kinds, ranks_local) + (2,) * tensor_bits + (units_here,)
        )
        for bit in range(tensor_bits):
            keep, send = halve(second, "tensor", bit, second.ndim - 2)
            got = swap(send, "tensor", bit)
            second = jnp.where(
                ((core >> bit) & 1) == 0,
                jnp.concatenate([keep, got], axis=2),
                jnp.concatenate([got, keep], axis=2),
            )
        hidden_blocks = []
        for block in range(NBLK):
            page = second[block]
            rows = slice(step * total_rows + block * BLK, step * total_rows + (block + 1) * BLK)
            gate, up = [
                main[kind][rows]
                + jnp.dot(
                    jnp.concatenate(
                        [part[rows, kind * rank : (kind + 1) * rank] for part in (high, low)], axis=1
                    ),
                    jnp.concatenate([page[kind], page[kind]], axis=0),
                    preferred_element_type=jnp.float32,
                )
                for kind in range(kinds)
            ]
            hidden_blocks.append((jax.nn.silu(gate) * up).astype(jnp.bfloat16))
        hidden = gather(jnp.concatenate(hidden_blocks, axis=0), "tensor", 1)
        parts = [
            jnp.dot(
                hidden,
                down_weight[:, piece * half : (piece + 1) * half],
                preferred_element_type=jnp.float32,
            ).reshape((2,) * bits + (rows_here, half))
            for piece in range(2)
        ]
        pairs = [
            halve(parts[piece], "pool", orders[piece][0], bits - 1 - orders[piece][0], jnp.bfloat16)
            for piece in range(2)
        ]
        sends = [send for _, send in pairs]
        if arrived is not None:
            sends, _ = lax.optimization_barrier((sends, arrived))
        arrived = [swap(sends[piece], "pool", orders[piece][0]) for piece in range(2)]
        sums.append([pairs[piece][0] + arrived[piece].astype(jnp.float32) for piece in range(2)])
    results = []
    for step in range(steps):
        pieces = []
        for piece in range(2):
            current = sums[step][piece]
            remaining = list(reversed(range(bits)))
            remaining.remove(orders[piece][0])
            for bit in orders[piece][1:]:
                keep, send = halve(current, "pool", bit, remaining.index(bit), jnp.bfloat16)
                remaining.remove(bit)
                current = keep + swap(send, "pool", bit).astype(jnp.float32)
            pieces.append(current)
        live = jnp.sum(
            (owners[:, None] == jnp.arange(NBLK)[None, :]) * block_live[step][None, :], axis=1
        )
        keep = (positions % BLK < live).astype(jnp.float32)
        summed = jnp.concatenate(pieces, axis=1)
        results.append((summed * keep[:, None]).astype(jnp.bfloat16))
    return jnp.stack(results)


def solution(mesh):
    return jax.shard_map(
        shards,
        mesh=mesh,
        in_specs=(
            P(None, None, "tensor"),
            P("tensor", None, "pool"),
            P("pool", "tensor"),
            P("pool", None, "tensor", None),
            P("pool", None, "tensor", None),
            P(),
            P(),
            P(),
        ),
        out_specs=P(None, "pool", "tensor"),
        check_vma=False,
    )
```

time: 254 us -> 227 us (0.89)
  waiting for transfers between devices: 117 us -> 46.3 us
  starting transfers between devices: 26.4 us -> 55.9 us
  local copies, waits for them, and re-layouts: 31.8 us -> 50.7 us
  other arithmetic: 8.27 us -> 23.6 us
  between operations: 23.1 us -> 10.8 us
  matrix products: 46.2 us -> 38.5 us
    psum x1 -> x0, waiting for transfers between devices: 77.6 us -> none  [shards(): shrunk = lax.psum(first * mine[:, :, None, None], ('pool', 'tensor'))]
    ppermute x16 -> x42, starting transfers between devices: 18.8 us -> 55.9 us  [the longest x36 46.9 us: swap(): return lax.ppermute(array, axis_name, bit_pairs(axis_name, bit))]
    optimization_barrier x0 -> x1, local copies, waits for them, and re-layouts: none -> 20.3 us  [after(): return lax.optimization_barrier((array, arrived))[0]]
    ppermute x16 -> x42, waiting for transfers between devices: 31 us -> 46.3 us  [the longest x36 31.3 us: swap(): return lax.ppermute(array, axis_name, bit_pairs(axis_name, bit))]
    unnamed x24 -> x51, local copies, waits for them, and re-layouts: 23.1 us -> 7.92 us
    another operation x0 -> x12, local copies, waits for them, and re-layouts: none -> 10 us  [plane_pages(): sends.append(jnp.stack([send for _, send in split.values()]))]
    all_gather x1 -> x0, waiting for transfers between devices: 8.73 us -> none  [shards(): lax.all_gather(jnp.concatenate(hidden_blocks, axis=0), 'tensor', axis=1,...]
    select_n x0 -> x13, other arithmetic: none -> 8.43 us  [the longest x8 7.88 us: plane_exchange(): lax.select_n(choice, *[one[kind] for one in columns])]
  transfers between devices with their start and end apart: 20 -> 42, of which waited for: 12 -> 18; matrix products, arithmetic and copies ran while one was open for 26% -> 45% of each run, Pallas kernels for 0% -> 0%
where the time goes in v2:
time: 227 us; the launch traced here: 226 us
  starting transfers between devices  55.9 us (25%)
  local copies, waits for them, and re-layouts  50.7 us (22%)
  waiting for transfers between devices  46.3 us (20%)
  matrix products  38.5 us (17%)
  other arithmetic  23.6 us (10%)
  between operations  10.8 us (5%)
    ppermute x36, starting transfers between devices, swap(): return lax.ppermute(array, axis_name, bit_pairs(axis_name, bit))  46.9 us
    ppermute x36, waiting for transfers between devices, swap(): return lax.ppermute(array, axis_name, bit_pairs(axis_name, bit))  31.3 us
    dot_general x2, matrix products, shards(): jnp.dot(flat_tokens, weights[kind], preferred_element_type=jnp.float32)  20.7 us
    optimization_barrier x1, local copies, waits for them, and re-layouts, after(): return lax.optimization_barrier((array, arrived))[0]  20.3 us
    ppermute x6, waiting for transfers between devices, plane_exchange(): picked = lax.ppermute(picked, 'pool', pairs)  14.9 us
    dot_general x4, matrix products, shards(): jnp.dot(hidden, down_weight[:, piece * half:(piece + 1) * half], preferre...  11.8 us
    another operation x12, local copies, waits for them, and re-layouts, plane_pages(): sends.append(jnp.stack([send for _, send in split.values()]))  10 us
    ppermute x6, starting transfers between devices, plane_exchange(): picked = lax.ppermute(picked, 'pool', pairs)  9.02 us
  transfers between devices with their start and end apart: 42, of which 18 were waited for; matrix products, arithmetic and copies ran while one was open for 45% of the time, Pallas kernels for 0%

profile of v2, /device:TPU:0, one launch (start us, length us, event | category | flops | bytes accessed | tf_op | source)
XLA Modules:
  0.0 226.0 jit_solution(9443635925535515903)
XLA Ops:
  0.0 2.8 %copy.73 = bf16[8,8,16,1792]{3,2,1,0:T(8,128)(2,1)S(1)} copy(bf16[8,8,16,1792]{3,1,2,0:T(8,128)(2,1)} %bitcast.839) | data formatting | bytes 7340032
  5.4 3.0 %collective-permute-start.8 = (bf16[1,16,4,2,1792]{4,1,3,2,0:T(8,128)(2,1)}, bf16[1,16,4,2,1792]{4,1,3,2,0:T(8,128)(2,1)S(1)}, u32[]{:S(2)}, u32[]{:S(2)}) collective-permute-start(bf16[1,16,4,2,1792]{4,1,3,2,0:T(8,128)(2,1)} %dynamic-slice_bitcast_fusion.2), channel_id=1, source_target_pairs={{0,4},{2,6},{4,0},{6,2},{8,12},{10,14},{12,8},{14,10},{16,20},{18,... | collective-permute-start | bytes 1376264 | tf_op jit(solution)/shard_map/ppermute | solution.py:24
  13.1 3.7 %fusion.30 = f32[2,256,2,64]{1,3,2,0:T(8,128)S(1)} fusion(bf16[2,256,4096]{2,1,0:T(8,128)(2,1)} %param.10, bf16[1,2,4096,64]{2,3,1,0:T(8,128)(2,1)S(1)} %copy-done, f32[2,256]{1,0:T(2,128)S(1)} %bitcast.852), kind=kOutput, calls=%fused_computation.139 | convolution fusion | flops 536936448 | bytes 5507072 | tf_op jit(solution)/shard_map/snd,kdc->snkc/dot_general | solution.py:203
  31.1 4.0 %collective-permute-done.23 = f32[256,128]{0,1:T(8,128)} collective-permute-done((f32[256,128]{0,1:T(8,128)S(1)}, f32[256,128]{0,1:T(8,128)}, u32[]{:S(2)}, u32[]{:S(2)}) %collective-permute-start.23) | collective-permute-done | bytes 131104 | tf_op jit(solution)/shard_map/ppermute | solution.py:24
  46.4 2.7 %collective-permute-start.26 = (f32[256,128]{0,1:T(8,128)S(1)}, f32[256,128]{0,1:T(8,128)}, u32[]{:S(2)}, u32[]{:S(2)}) collective-permute-start(f32[256,128]{0,1:T(8,128)S(1)} %add.874), channel_id=1, source_target_pairs={{0,16},{2,18},{4,20},{6,22},{8,24},{10,26},{12,28},{14,30},{16,0},... | collective-permute-start | bytes 393224 | tf_op jit(solution)/shard_map/ppermute | solution.py:24
  64.6 20.3 %copy.99 = bf16[4096,2,1792]{2,0,1:T(8,128)(2,1)} copy(bf16[4096,2,1792]{2,1,0:T(2,128)(2,1)} %param.11) | data formatting | bytes 58720256 | tf_op jit(solution)/shard_map/optimization_barrier | solution.py:65
  92.2 3.7 %collective-permute-start.18 = (bf16[2,2,16,1792]{3,2,1,0:T(8,128)(2,1)S(1)}, bf16[2,2,16,1792]{3,2,1,0:T(8,128)(2,1)S(1)}, u32[]{:S(2)}, u32[]{:S(2)}) collective-permute-start(bf16[2,2,16,1792]{3,2,1,0:T(8,128)(2,1)S(1)} %pad_maximum_fusion.18), channel_id=1, source_target_pairs={{0,24},{2,26},{4,28},{6,30},{8,16},{10,18},{12,20},{14,22},{16,8},... | collective-permute-start | bytes 688136 | tf_op jit(solution)/shard_map/ppermute | solution.py:127
  99.1 10.4 %fusion.19 = f32[512,1792]{1,0:T(8,128)S(1)} fusion(bf16[512,4096]{1,0:T(8,128)(2,1)S(1)} %bitcast.855, bf16[2,4096,1792]{2,1,0:T(8,128)(2,1)} %bitcast.816), kind=kOutput, calls=%fused_computation.123 | convolution fusion | flops 7516192768 | bytes 22544384 | tf_op jit(solution)/shard_map/dot_general | solution.py:221
  109.8 10.4 %fusion.18 = f32[512,1792]{1,0:T(8,128)S(1)} fusion(bf16[512,4096]{1,0:T(8,128)(2,1)S(1)} %bitcast.856, bf16[2,4096,1792]{2,1,0:T(8,128)(2,1)} %bitcast.817), kind=kOutput, calls=%fused_computation.121 | convolution fusion | flops 7516192768 | bytes 22544384 | tf_op jit(solution)/shard_map/dot_general | solution.py:221
  128.0 3.2 %collective-permute-start.19 = (bf16[2,2,16,1792]{3,2,1,0:T(8,128)(2,1)S(1)}, bf16[2,2,16,1792]{3,2,1,0:T(8,128)(2,1)S(1)}, u32[]{:S(2)}, u32[]{:S(2)}) collective-permute-start(bf16[2,2,16,1792]{3,2,1,0:T(8,128)(2,1)S(1)} %pad_maximum_fusion.19), channel_id=1, source_target_pairs={{0,24},{2,26},{4,28},{6,30},{8,16},{10,18},{12,20},{14,22},{16,8},... | collective-permute-start | bytes 688136 | tf_op jit(solution)/shard_map/ppermute | solution.py:127
  131.2 6.1 %collective-permute-done.15 = bf16[2,2,16,1792]{3,2,1,0:T(8,128)(2,1)S(1)} collective-permute-done((bf16[2,2,16,1792]{3,2,1,0:T(8,128)(2,1)S(1)}, bf16[2,2,16,1792]{3,2,1,0:T(8,128)(2,1)S(1)}, u32[]{:S(2)}, u32[]{:S(2)}) %collective-permute-start.15) | collective-permute-done | bytes 229408 | tf_op jit(solution)/shard_map/ppermute | solution.py:127
  137.3 8.9 %collective-permute-done.17 = bf16[2,2,16,1792]{3,2,1,0:T(8,128)(2,1)S(1)} collective-permute-done((bf16[2,2,16,1792]{3,2,1,0:T(8,128)(2,1)S(1)}, bf16[2,2,16,1792]{3,2,1,0:T(8,128)(2,1)S(1)}, u32[]{:S(2)}, u32[]{:S(2)}) %collective-permute-start.17) | collective-permute-done | bytes 229408 | tf_op jit(solution)/shard_map/ppermute | solution.py:127
  149.5 2.5 %conditional.1 = (bf16[4,2,32,1792]{3,2,1,0:T(8,128)(2,1)S(1)}, bf16[2,2,32,1792]{3,2,1,0:T(8,128)(2,1)}, bf16[2,2,32,1792]{3,2,1,0:T(8,128)(2,1)}, bf16[2,2,32,...) conditional(s32[]{:T(128)} %convert_element_type.215, ...), branch_computations={%region_5.6_spmd, %region_6.9_spmd} | conditional | flops 24543300 | bytes 30279052 | solution.py:237
  157.9 5.5 %fusion.26 = f32[256,2048]{1,0:T(8,128)S(1)} fusion(bf16[1792,4096]{1,0:T(8,128)(2,1)} %param.12, bf16[256,896]{1,0:T(8,128)(2,1)S(1)} %collective-permute-done.29, bf16[128,896]{1,0:T(8,128)(2,1)S(1)} %multiply_convert_fusion.2, bf16[128,896]{1,0:T(8,128)(2,1)S(1)} %multiply_convert_fusion.3, pred[]{:T(512)S(6)} %eq.35), kind=kOutput, calls=%fused_computation.130 | convolution fusion | flops 1885011968 | bytes 10354689 | tf_op jit(solution)/shard_map/dot_general | solution.py:279
  165.0 2.1 fusion.22
  168.8 2.1 fusion.20
  170.9 2.1 fusion.24
  173.2 5.1 %collective-permute-done.30 = bf16[2,2,2,16,2048]{4,3,0,1,2:T(8,128)(2,1)S(1)} collective-permute-done((bf16[2,2,2,16,2048]{4,3,0,1,2:T(8,128)(2,1)S(1)}, bf16[2,2,2,16,2048]{4,3,0,1,2:T(8,128)(2,1)S(1)}, u32[]{:S(2)}, u32[]{:S(2)}) %collective-permute-start.30) | collective-permute-done | bytes 524320 | tf_op jit(solution)/shard_map/ppermute | solution.py:24
  187.9 4.6 %collective-permute-start.32 = (bf16[2,16,2048]{2,1,0:T(8,128)(2,1)S(1)}, bf16[2,16,2048]{2,1,0:T(8,128)(2,1)S(1)}, u32[]{:S(2)}, u32[]{:S(2)}) collective-permute-start(bf16[2,16,2048]{2,1,0:T(8,128)(2,1)S(1)} %fusion.85), channel_id=1, source_target_pairs={{0,8},{2,10},{4,12},{6,14},{8,0},{10,2},{12,4},{14,6},{16,24},{18,... | collective-permute-start | bytes 393224 | tf_op jit(solution)/shard_map/ppermute | solution.py:24
  192.6 3.7 %collective-permute-start.36 = (bf16[2,16,2048]{2,1,0:T(8,128)(2,1)S(1)}, bf16[2,16,2048]{2,1,0:T(8,128)(2,1)S(1)}, u32[]{:S(2)}, u32[]{:S(2)}) collective-permute-start(bf16[2,16,2048]{2,1,0:T(8,128)(2,1)S(1)} %fusion.86), channel_id=1, source_target_pairs={{0,8},{2,10},{4,12},{6,14},{8,0},{10,2},{12,4},{14,6},{16,24},{18,... | collective-permute-start | bytes 393224 | tf_op jit(solution)/shard_map/ppermute | solution.py:24
  196.8 2.1 collective-permute-start.33
  202.8 2.4 %collective-permute-done.37 = bf16[16,2048]{1,0:T(8,128)(2,1)S(1)} collective-permute-done((bf16[16,2048]{1,0:T(8,128)(2,1)S(1)}, bf16[16,2048]{1,0:T(8,128)(2,1)S(1)}, u32[]{:S(2)}, u32[]{:S(2)}) %collective-permute-start.37) | collective-permute-done | bytes 65568 | tf_op jit(solution)/shard_map/ppermute | solution.py:24
  207.7 4.3 %collective-permute-done.41 = bf16[2,2,16,2048]{3,2,0,1:T(8,128)(2,1)S(1)} collective-permute-done((bf16[2,2,16,2048]{3,2,0,1:T(8,128)(2,1)S(1)}, bf16[2,2,16,2048]{3,2,0,1:T(8,128)(2,1)S(1)}, u32[]{:S(2)}, u32[]{:S(2)}) %collective-permute-start.41) | collective-permute-done | bytes 262176 | tf_op jit(solution)/shard_map/ppermute | solution.py:24
  215.1 2.7 %collective-permute-done.42 = bf16[2,16,2048]{2,1,0:T(8,128)(2,1)S(1)} collective-permute-done((bf16[2,16,2048]{2,1,0:T(8,128)(2,1)S(1)}, bf16[2,16,2048]{2,1,0:T(8,128)(2,1)S(1)}, u32[]{:S(2)}, u32[]{:S(2)}) %collective-permute-start.42) | collective-permute-done | bytes 131104 | tf_op jit(solution)/shard_map/ppermute | solution.py:24
  (262 shorter events, 99.4 us)
Async XLA Ops:
  5.4 37.4 %collective-permute-start.8 = (bf16[1,16,4,2,1792]{4,1,3,2,0:T(8,128)(2,1)}, bf16[1,16,4,2,1792]{4,1,3,2,0:T(8,128)(2,1)S(1)}, u32[]{:S(2)}, u32[]{:S(2)}) collective-permute-start(bf16[1,16,4,2,1792]{4,1,3,2,0:T(8,128)(2,1)} %dynamic-slice_bitcast_fusion.2), channel_id=1, source_target_pairs={{0,4},{2,6},{4,0},{6,2},{8,12},{10,14},{12,8},{14,10},{16,20},{18,... | collective-permute-start | bytes 1376264 | tf_op jit(solution)/shard_map/ppermute | solution.py:24
  10.7 34.7 %collective-permute-start.6 = (bf16[1,16,4,2,1792]{4,1,3,2,0:T(8,128)(2,1)}, bf16[1,16,4,2,1792]{4,1,3,2,0:T(8,128)(2,1)}, u32[]{:S(2)}, u32[]{:S(2)}) collective-permute-start(bf16[1,16,4,2,1792]{4,1,3,2,0:T(8,128)(2,1)} %dynamic-slice_bitcast_fusion.3), channel_id=1, source_target_pairs={{0,2},{2,0},{4,6},{6,4},{8,10},{10,8},{12,14},{14,12},{16,18},{18,... | collective-permute-start | bytes 1376264 | tf_op jit(solution)/shard_map/ppermute | solution.py:24
  17.5 10.6 %collective-permute-start.22 = (f32[256,128]{0,1:T(8,128)S(1)}, f32[256,128]{0,1:T(8,128)}, u32[]{:S(2)}, u32[]{:S(2)}) collective-permute-start(f32[256,128]{0,1:T(8,128)S(1)} %dynamic-slice_bitcast_fusion.16), channel_id=1, source_target_pairs={{0,1},{1,0},{2,3},{3,2},{4,5},{5,4},{6,7},{7,6},{8,9},{9,8},{10,11... | collective-permute-start | bytes 393224 | tf_op jit(solution)/shard_map/ppermute | solution.py:24
  44.8 15.8 %collective-permute-start.9 = (bf16[2,16,4,1792]{3,1,2,0:T(8,128)(2,1)}, bf16[2,16,4,1792]{3,1,2,0:T(8,128)(2,1)}, u32[]{:S(2)}, u32[]{:S(2)}) collective-permute-start(bf16[2,16,4,1792]{3,1,2,0:T(8,128)(2,1)} %pad_maximum_fusion.8), channel_id=1, source_target_pairs={{0,2},{2,0},{4,6},{6,4},{8,10},{10,8},{12,14},{14,12},{16,18},{18,... | collective-permute-start | bytes 1376264 | tf_op jit(solution)/shard_map/ppermute | solution.py:24
  46.4 11.2 %collective-permute-start.26 = (f32[256,128]{0,1:T(8,128)S(1)}, f32[256,128]{0,1:T(8,128)}, u32[]{:S(2)}, u32[]{:S(2)}) collective-permute-start(f32[256,128]{0,1:T(8,128)S(1)} %add.874), channel_id=1, source_target_pairs={{0,16},{2,18},{4,20},{6,22},{8,24},{10,26},{12,28},{14,30},{16,0},... | collective-permute-start | bytes 393224 | tf_op jit(solution)/shard_map/ppermute | solution.py:24
  50.8 10.8 %collective-permute-start.7 = (bf16[2,16,4,1792]{3,1,2,0:T(8,128)(2,1)}, bf16[2,16,4,1792]{3,1,2,0:T(8,128)(2,1)}, u32[]{:S(2)}, u32[]{:S(2)}) collective-permute-start(bf16[2,16,4,1792]{3,1,2,0:T(8,128)(2,1)} %pad_maximum_fusion.7), channel_id=1, source_target_pairs={{0,4},{2,6},{4,0},{6,2},{8,12},{10,14},{12,8},{14,10},{16,20},{18,... | collective-permute-start | bytes 1376264 | tf_op jit(solution)/shard_map/ppermute | solution.py:24
  61.6 34.3 %collective-permute-start.10 = (bf16[1,16,4,2,1792]{4,1,3,2,0:T(8,128)(2,1)}, bf16[1,16,4,2,1792]{4,1,3,2,0:T(8,128)(2,1)}, u32[]{:S(2)}, u32[]{:S(2)}) collective-permute-start(bf16[1,16,4,2,1792]{4,1,3,2,0:T(8,128)(2,1)} %dynamic-slice_bitcast_fusion.1), channel_id=1, source_target_pairs={{0,2},{2,0},{4,6},{6,4},{8,10},{10,8},{12,14},{14,12},{16,18},{18,... | collective-permute-start | bytes 1376264 | tf_op jit(solution)/shard_map/ppermute | solution.py:24
  63.1 32.8 %collective-permute-start.12 = (bf16[1,16,4,2,1792]{4,1,3,2,0:T(8,128)(2,1)}, bf16[1,16,4,2,1792]{4,1,3,2,0:T(8,128)(2,1)}, u32[]{:S(2)}, u32[]{:S(2)}) collective-permute-start(bf16[1,16,4,2,1792]{4,1,3,2,0:T(8,128)(2,1)} %dynamic-slice_bitcast_fusion), channel_id=1, source_target_pairs={{0,4},{2,6},{4,0},{6,2},{8,12},{10,14},{12,8},{14,10},{16,20},{18,... | collective-permute-start | bytes 1376264 | tf_op jit(solution)/shard_map/ppermute | solution.py:24
  89.3 37.5 %collective-permute-start.14 = (bf16[2,2,16,1792]{3,2,1,0:T(8,128)(2,1)S(1)}, bf16[2,2,16,1792]{3,2,1,0:T(8,128)(2,1)S(1)}, u32[]{:S(2)}, u32[]{:S(2)}) collective-permute-start(bf16[2,2,16,1792]{3,2,1,0:T(8,128)(2,1)S(1)} %pad_maximum_fusion.14), channel_id=1, source_target_pairs={{0,8},{2,10},{4,12},{6,14},{8,0},{10,2},{12,4},{14,6},{16,24},{18,... | collective-permute-start | bytes 688136 | tf_op jit(solution)/shard_map/ppermute | solution.py:127
  89.8 37.0 %collective-permute-start.16 = (bf16[2,2,16,1792]{3,2,1,0:T(8,128)(2,1)S(1)}, bf16[2,2,16,1792]{3,2,1,0:T(8,128)(2,1)S(1)}, u32[]{:S(2)}, u32[]{:S(2)}) collective-permute-start(bf16[2,2,16,1792]{3,2,1,0:T(8,128)(2,1)S(1)} %pad_maximum_fusion.16), channel_id=1, source_target_pairs={{0,16},{2,18},{4,20},{6,22},{8,24},{10,26},{12,28},{14,30},{16,0},... | collective-permute-start | bytes 688136 | tf_op jit(solution)/shard_map/ppermute | solution.py:127
  92.2 35.8 %collective-permute-start.18 = (bf16[2,2,16,1792]{3,2,1,0:T(8,128)(2,1)S(1)}, bf16[2,2,16,1792]{3,2,1,0:T(8,128)(2,1)S(1)}, u32[]{:S(2)}, u32[]{:S(2)}) collective-permute-start(bf16[2,2,16,1792]{3,2,1,0:T(8,128)(2,1)S(1)} %pad_maximum_fusion.18), channel_id=1, source_target_pairs={{0,24},{2,26},{4,28},{6,30},{8,16},{10,18},{12,20},{14,22},{16,8},... | collective-permute-start | bytes 688136 | tf_op jit(solution)/shard_map/ppermute | solution.py:127
  96.9 12.8 %collective-permute-start.11 = (bf16[2,16,4,1792]{3,1,2,0:T(8,128)(2,1)S(1)}, bf16[2,16,4,1792]{3,1,2,0:T(8,128)(2,1)S(1)}, u32[]{:S(2)}, u32[]{:S(2)}) collective-permute-start(bf16[2,16,4,1792]{3,1,2,0:T(8,128)(2,1)S(1)} %pad_maximum_fusion.9), channel_id=1, source_target_pairs={{0,4},{2,6},{4,0},{6,2},{8,12},{10,14},{12,8},{14,10},{16,20},{18,... | collective-permute-start | bytes 1376264 | tf_op jit(solution)/shard_map/ppermute | solution.py:24
  98.5 11.3 %collective-permute-start.13 = (bf16[2,16,4,1792]{3,1,2,0:T(8,128)(2,1)S(1)}, bf16[2,16,4,1792]{3,1,2,0:T(8,128)(2,1)S(1)}, u32[]{:S(2)}, u32[]{:S(2)}) collective-permute-start(bf16[2,16,4,1792]{3,1,2,0:T(8,128)(2,1)S(1)} %pad_maximum_fusion.10), channel_id=1, source_target_pairs={{0,2},{2,0},{4,6},{6,4},{8,10},{10,8},{12,14},{14,12},{16,18},{18,... | collective-permute-start | bytes 1376264 | tf_op jit(solution)/shard_map/ppermute | solution.py:24
  109.7 36.9 %collective-permute-start.20 = (f32[512,896]{1,0:T(8,128)S(1)}, f32[512,896]{1,0:T(8,128)S(1)}, u32[]{:S(2)}, u32[]{:S(2)}) collective-permute-start(f32[512,896]{1,0:T(8,128)S(1)} %slice_select_fusion.1), channel_id=1, source_target_pairs={{0,1},{1,0},{2,3},{3,2},{4,5},{5,4},{6,7},{7,6},{8,9},{9,8},{10,11... | collective-permute-start | bytes 5505032 | tf_op jit(solution)/shard_map/ppermute | solution.py:24
  120.3 27.7 %collective-permute-start.21 = (f32[512,896]{1,0:T(8,128)S(1)}, f32[512,896]{1,0:T(8,128)S(1)}, u32[]{:S(2)}, u32[]{:S(2)}) collective-permute-start(f32[512,896]{1,0:T(8,128)S(1)} %slice_select_fusion), channel_id=1, source_target_pairs={{0,1},{1,0},{2,3},{3,2},{4,5},{5,4},{6,7},{7,6},{8,9},{9,8},{10,11... | collective-permute-start | bytes 5505032 | tf_op jit(solution)/shard_map/ppermute | solution.py:24
  126.7 10.5 %collective-permute-start.15 = (bf16[2,2,16,1792]{3,2,1,0:T(8,128)(2,1)S(1)}, bf16[2,2,16,1792]{3,2,1,0:T(8,128)(2,1)S(1)}, u32[]{:S(2)}, u32[]{:S(2)}) collective-permute-start(bf16[2,2,16,1792]{3,2,1,0:T(8,128)(2,1)S(1)} %pad_maximum_fusion.15), channel_id=1, source_target_pairs={{0,8},{2,10},{4,12},{6,14},{8,0},{10,2},{12,4},{14,6},{16,24},{18,... | collective-permute-start | bytes 688136 | tf_op jit(solution)/shard_map/ppermute | solution.py:127
  126.8 19.3 %collective-permute-start.17 = (bf16[2,2,16,1792]{3,2,1,0:T(8,128)(2,1)S(1)}, bf16[2,2,16,1792]{3,2,1,0:T(8,128)(2,1)S(1)}, u32[]{:S(2)}, u32[]{:S(2)}) collective-permute-start(bf16[2,2,16,1792]{3,2,1,0:T(8,128)(2,1)S(1)} %pad_maximum_fusion.17), channel_id=1, source_target_pairs={{0,16},{2,18},{4,20},{6,22},{8,24},{10,26},{12,28},{14,30},{16,0},... | collective-permute-start | bytes 688136 | tf_op jit(solution)/shard_map/ppermute | solution.py:127
  128.0 18.1 %collective-permute-start.19 = (bf16[2,2,16,1792]{3,2,1,0:T(8,128)(2,1)S(1)}, bf16[2,2,16,1792]{3,2,1,0:T(8,128)(2,1)S(1)}, u32[]{:S(2)}, u32[]{:S(2)}) collective-permute-start(bf16[2,2,16,1792]{3,2,1,0:T(8,128)(2,1)S(1)} %pad_maximum_fusion.19), channel_id=1, source_target_pairs={{0,24},{2,26},{4,28},{6,30},{8,16},{10,18},{12,20},{14,22},{16,8},... | collective-permute-start | bytes 688136 | tf_op jit(solution)/shard_map/ppermute | solution.py:127
  157.8 11.0 %collective-permute-start.39 = (bf16[256,896]{1,0:T(8,128)(2,1)S(1)}, bf16[256,896]{1,0:T(8,128)(2,1)S(1)}, u32[]{:S(2)}, u32[]{:S(2)}) collective-permute-start(bf16[256,896]{1,0:T(8,128)(2,1)S(1)} %pad_maximum_fusion.12), channel_id=1, source_target_pairs={{0,1},{1,0},{2,3},{3,2},{4,5},{5,4},{6,7},{7,6},{8,9},{9,8},{10,11... | collective-permute-start | bytes 1376264 | tf_op jit(solution)/shard_map/ppermute | solution.py:24
  163.4 14.9 %collective-permute-start.30 = (bf16[2,2,2,16,2048]{4,3,0,1,2:T(8,128)(2,1)S(1)}, bf16[2,2,2,16,2048]{4,3,0,1,2:T(8,128)(2,1)S(1)}, u32[]{:S(2)}, u32[]{:S(2)}) collective-permute-start(bf16[2,2,2,16,2048]{4,3,0,1,2:T(8,128)(2,1)S(1)} %fusion.34), channel_id=1, source_target_pairs={{0,2},{2,0},{4,6},{6,4},{8,10},{10,8},{12,14},{14,12},{16,18},{18,... | collective-permute-start | bytes 1572872 | tf_op jit(solution)/shard_map/ppermute | solution.py:24
  167.2 14.9 %collective-permute-start.34 = (bf16[2,2,2,16,2048]{4,3,0,1,2:T(8,128)(2,1)S(1)}, bf16[2,2,2,16,2048]{4,3,0,1,2:T(8,128)(2,1)S(1)}, u32[]{:S(2)}, u32[]{:S(2)}) collective-permute-start(bf16[2,2,2,16,2048]{4,3,0,1,2:T(8,128)(2,1)S(1)} %fusion.35), channel_id=1, source_target_pairs={{0,4},{2,6},{4,0},{6,2},{8,12},{10,14},{12,8},{14,10},{16,20},{18,... | collective-permute-start | bytes 1572872 | tf_op jit(solution)/shard_map/ppermute | solution.py:24
  182.2 10.3 %collective-permute-start.35 = (bf16[2,2,16,2048]{3,2,0,1:T(8,128)(2,1)S(1)}, bf16[2,2,16,2048]{3,2,0,1:T(8,128)(2,1)S(1)}, u32[]{:S(2)}, u32[]{:S(2)}) collective-permute-start(bf16[2,2,16,2048]{3,2,0,1:T(8,128)(2,1)S(1)} %fusion.39), channel_id=1, source_target_pairs={{0,2},{2,0},{4,6},{6,4},{8,10},{10,8},{12,14},{14,12},{16,18},{18,... | collective-permute-start | bytes 786440 | tf_op jit(solution)/shard_map/ppermute | solution.py:24
  182.5 22.7 %collective-permute-start.40 = (bf16[2,2,2,16,2048]{4,3,0,1,2:T(8,128)(2,1)S(1)}, bf16[2,2,2,16,2048]{4,3,0,1,2:T(8,128)(2,1)S(1)}, u32[]{:S(2)}, u32[]{:S(2)}) collective-permute-start(bf16[2,2,2,16,2048]{4,3,0,1,2:T(8,128)(2,1)S(1)} %fusion.36), channel_id=1, source_target_pairs={{0,2},{2,0},{4,6},{6,4},{8,10},{10,8},{12,14},{14,12},{16,18},{18,... | collective-permute-start | bytes 1572872 | tf_op jit(solution)/shard_map/ppermute | solution.py:24
  184.3 22.8 %collective-permute-start.44 = (bf16[2,2,2,16,2048]{4,3,0,1,2:T(8,128)(2,1)S(1)}, bf16[2,2,2,16,2048]{4,3,0,1,2:T(8,128)(2,1)S(1)}, u32[]{:S(2)}, u32[]{:S(2)}) collective-permute-start(bf16[2,2,2,16,2048]{4,3,0,1,2:T(8,128)(2,1)S(1)} %fusion.37), channel_id=1, source_target_pairs={{0,4},{2,6},{4,0},{6,2},{8,12},{10,14},{12,8},{14,10},{16,20},{18,... | collective-permute-start | bytes 1572872 | tf_op jit(solution)/shard_map/ppermute | solution.py:24
  (40 other events, 345.5 us)
